TPU v7x, 256 devices: a whole 4x4x8 slice. The times are simulated.
256 devices in a mesh: gx: 16 (over y, x), gy: 16 (over z, core).
Axes of the slice: x: 4, y: 4, z: 8, core: 2. Of those that a mesh axis runs over, the one named last changes fastest.
Arguments:
- field: float32 [768, 768, 256], P('gx', 'gy'), may hold values from -6 to 6
- stdev: float32 [768, 768, 256], P('gx', 'gy'), may hold values from 0.5 to 2
- mixing: float32 [4, 256, 256], replicated, may hold values from -0.375 to 0.375
- gen_weight: float32 [4, 256], replicated, may hold values from 0.5 to 4
Outputs:
- covariance_product: float32 [768, 768, 256], P('gx', 'gy')
All inputs are finite; a program needn't handle non-finite values.
Results may differ from a plain program's by a relative error of at most 0.0001.
Values sent between devices are 32-bit elements; how exact they have to be, the bound alone decides.
A program may use at most 128 MiB of HBM per device.

v0:
```python
import functools

import jax
import jax.numpy as jnp
from jax import lax
from jax.experimental import pallas as pl
from jax.experimental.pallas import tpu as pltpu
from jax.sharding import PartitionSpec as P

RAD = 3
GENS = 4
LANE = 128
MESH = pl.DeviceIdType.MESH
DIRS = [(1, 0), (-1, 0), (0, 1), (0, -1), (1, 1), (1, -1), (-1, 1), (-1, -1)]
N = (48, 24, 12, 6)
RIM = (3, 5, 6, 6)
OUT = (0, 2, 3, 3)
YO = 8

_total = sum((1.0 - (k / (RAD + 1.0)) ** 2) ** 2 for k in range(-RAD, RAD + 1))
B = [(1.0 - (k / (RAD + 1.0)) ** 2) ** 2 / _total for k in range(RAD + 1)]
DOWN = [B[3], B[2] + B[3], B[1] + B[2], B[0] + B[1], B[0] + B[1], B[1] + B[2], B[2] + B[3], B[3]]
EVEN = [B[3], B[1] + B[2], B[0] + B[1], B[2] + B[3]]
ODD = EVEN[::-1]


def loop(count, step, unroll=1):
    def one(i, carry):
        step(i)
        return carry

    lax.fori_loop(0, count, one, 0, unroll=unroll)


def filtered(load):
    return load(3) * B[0] + (load(2) + load(4)) * B[1] + (load(1) + load(5)) * B[2] + (load(0) + load(6)) * B[3]


def restricted(load):
    return (
        (load(3) + load(4)) * DOWN[3]
        + (load(2) + load(5)) * DOWN[2]
        + (load(1) + load(6)) * DOWN[1]
        + (load(0) + load(7)) * DOWN[0]
    )


def dotted(weights, parts, scale=1.0):
    total = parts[0] * (weights[0] * scale)
    for weight, part in zip(weights[1:], parts[1:]):
        total = total + part * (weight * scale)
    return total


def restrict_rows(src, first, count, cols, dst, rows, shift, dst_cols):
    whole = [i for i in range(rows) if 2 * i - shift >= 0 and 2 * i - shift + 7 < count]
    low, high = whole[0], whole[-1] + 1
    for half in range(2):
        for i in list(range(low)) + list(range(high, rows)):
            taps = [t for t in range(8) if 0 <= 2 * i - shift + t < count]
            parts = [src[first + 2 * i - shift + t, half, cols] for t in taps]
            dst[i, half, dst_cols] = dotted([DOWN[t] for t in taps], parts, 0.5)

    def step(j):
        for half in range(2):
            base = first + 2 * (j + low) - shift
            dst[j + low, half, dst_cols] = restricted(lambda t: src[base + t, half, cols]) * 0.5

    loop(high - low, step, 2)


def restrict_cols(src, start, dst, rows, cols):
    def step(i):
        for half in range(2):
            dst[i, half] = restricted(lambda t: src[i, half, pl.ds(start + t, cols, stride=2)])

    loop(rows, step, 2)


def filter_cols(src, start, dst, rows, cols):
    def step(i):
        for half in range(2):
            dst[i, half] = filtered(lambda t: src[i, half, pl.ds(start + t, cols)])

    loop(rows, step, 2)


def filter_rows(src, dst, rows):
    def step(i):
        for half in range(2):
            dst[i, half] = filtered(lambda t: src[i + t, half])

    loop(rows, step, 2)


def prolong_cols(src, dst, rows, count, odd_first):
    def step(i):
        for half in range(2):
            parts = [src[i, half, pl.ds(t, count)] for t in range(4 if odd_first else 5)]
            if odd_first:
                lead, next_one = dotted(ODD, parts), dotted(EVEN, parts)
            else:
                lead, next_one = dotted(EVEN, parts[:4]), dotted(ODD, parts[1:])
            dst[i, half, pl.ds(0, count, stride=2)] = lead
            dst[i, half, pl.ds(1, count, stride=2)] = next_one

    loop(rows, step, 2)


def prolong_rows(src, m, half, odd_first):
    parts = [src[m + t, half] for t in range(4 if odd_first else 5)]
    if odd_first:
        return dotted(ODD, parts, 0.5), dotted(EVEN, parts, 0.5)
    return dotted(EVEN, parts[:4], 0.5), dotted(ODD, parts[1:], 0.5)


def mix(ref, weights, gen, rows_each, steps, cols, unroll):
    count = rows_each * cols

    def step(i):
        rows = pl.ds(i * rows_each, rows_each)
        cells = jnp.concatenate([ref[rows, half].reshape(count, LANE) for half in range(2)], axis=1)
        high = cells.astype(jnp.bfloat16)
        low = (cells - high.astype(jnp.float32)).astype(jnp.bfloat16)
        product = jnp.dot(
            jnp.concatenate([high, high, low], axis=1), weights[gen], preferred_element_type=jnp.float32
        )
        for half in range(2):
            ref[rows, half] = product[:, half * LANE : (half + 1) * LANE].reshape(rows_each, cols, LANE)

    loop(steps, step, unroll)


def kernel(
    size_x, size_y, field, stdev, mixing, gen_weight, out,
    u0, u1, u2, u3, sd, mats, gains, weights,
    x1, x2, x3, c1, c2, c3,
    rx1, rx2, rx3, ry1, ry2, ry3, rc1, rc2, rc3,
    y0, y1, y2, y3, d0, d1, d2, d3, t1, t2, t3,
    load_sem, send_sem, recv_sem,
):
    gx, gy = lax.axis_index("gx"), lax.axis_index("gy")
    ext = (u0, u1, u2, u3)
    west, east = gx == 0, gx == size_x - 1
    south, north = gy == 0, gy == size_y - 1

    def there(d):
        nx, ny = gx + d[0], gy + d[1]
        return (nx >= 0) & (nx < size_x) & (ny >= 0) & (ny < size_y)

    def against(d):
        return (-d[0], -d[1])

    loads = []
    for part, (row, count) in enumerate(((0, 8), (40, 8), (8, 32))):
        for half in range(2):
            lanes = pl.ds(half * LANE, LANE)
            rows = pl.ds(row, count)
            loads.append(
                pltpu.make_async_copy(
                    field.at[rows, :, lanes], u0.at[pl.ds(row + RAD, count), half, pl.ds(YO, N[0])],
                    load_sem.at[part * 4 + half * 2],
                )
            )
            loads.append(
                pltpu.make_async_copy(
                    stdev.at[rows, :, lanes], sd.at[rows, half], load_sem.at[part * 4 + half * 2 + 1]
                )
            )
    loads.append(pltpu.make_async_copy(mixing, mats, load_sem.at[12]))
    loads.append(pltpu.make_async_copy(gen_weight, gains, load_sem.at[13]))
    for copy in loads:
        copy.start()

    barrier = pltpu.get_barrier_semaphore()
    for d in DIRS:

        @pl.when(there(d))
        def _():
            pl.semaphore_signal(barrier, inc=1, device_id=(gx + d[0], gy + d[1]), device_id_type=MESH)

    def gather_copy(gen, k):
        d, n, rim, buf = DIRS[k], N[gen], RIM[gen], ext[gen]

        def ranges(step, first):
            if step == 0:
                return pl.ds(first, n), pl.ds(first, n)
            if step > 0:
                return pl.ds(first + n - rim, rim), pl.ds(first - rim, rim)
            return pl.ds(first, rim), pl.ds(first + n, rim)

        (sx, tx), (sy, ty) = ranges(d[0], rim), ranges(d[1], YO)
        slot = gen * 8 + k
        return pltpu.make_async_remote_copy(
            src_ref=buf.at[sx, :, sy], dst_ref=buf.at[tx, :, ty],
            send_sem=send_sem.at[slot], recv_sem=recv_sem.at[slot],
            device_id=(gx + d[0], gy + d[1]), device_id_type=MESH,
        )

    def landing(gen, k):
        rx, ry, rc = ((rx1, ry1, rc1), (rx2, ry2, rc2), (rx3, ry3, rc3))[gen - 1]
        n, e = N[gen], OUT[gen]
        if k < 2:
            return rx.at[k, :, :, pl.ds(0, n)]
        if k < 4:
            return ry.at[k - 2, :, :, pl.ds(0, e)]
        return rc.at[k - 4, :, :, pl.ds(0, e)]

    def scatter_copy(gen, k):
        d, n, e, buf = DIRS[k], N[gen], OUT[gen], (c1, c2, c3)[gen - 1]

        def span(step):
            return pl.ds(e, n) if step == 0 else pl.ds(n + e, e) if step > 0 else pl.ds(0, e)

        slot = (gen + 3) * 8 + k
        return pltpu.make_async_remote_copy(
            src_ref=buf.at[span(d[0]), :, span(d[1])], dst_ref=landing(gen, k),
            send_sem=send_sem.at[slot], recv_sem=recv_sem.at[slot],
            device_id=(gx + d[0], gy + d[1]), device_id_type=MESH,
        )

    def start(make, gen, ks=range(8)):
        for k in ks:
            pl.when(there(DIRS[k]))(lambda k=k: make(gen, k).start())

    def arrive(make, gen):
        for k in range(8):
            pl.when(there(against(DIRS[k])))(lambda k=k: make(gen, k).wait_recv())

    def sent(make, gen):
        for k in range(8):
            pl.when(there(DIRS[k]))(lambda k=k: make(gen, k).wait_send())

    def clear(buf, rows, cols):
        loop(rows, lambda i: buf.__setitem__((i, slice(None), cols), jnp.zeros((2, cols.stop - cols.start, LANE), jnp.float32)))

    clear(x1, 28, slice(0, 8))
    clear(x1, 28, slice(56, 72))
    clear(x2, 18, slice(0, 8))
    clear(x2, 18, slice(40, 56))
    clear(x3, 12, slice(0, 8))
    clear(x3, 12, slice(32, 40))

    def clear_edges(buf, width, n, first_y, rows, whole_rows):
        cols = buf.shape[2]
        last = width + n

        def rows_at(first):
            for i in range(width):
                buf[first + i] = jnp.zeros((2, cols, LANE), jnp.float32)

        pl.when(west)(lambda: rows_at(0))
        pl.when(east)(lambda: rows_at(last))
        pl.when(south)(lambda: clear(buf, rows, slice(first_y - width, first_y)))
        pl.when(north)(lambda: clear(buf, rows, slice(first_y + n, first_y + n + width)))

    for gen in range(GENS):
        clear_edges(ext[gen], RIM[gen], N[gen], YO, N[gen] + 2 * RIM[gen], True)
    for gen in range(1, GENS):
        rx, ry, rc = ((rx1, ry1, rc1), (rx2, ry2, rc2), (rx3, ry3, rc3))[gen - 1]
        for k in range(8):
            buf, at = ((rx, k) if k < 2 else (ry, k - 2) if k < 4 else (rc, k - 4))

            @pl.when(jnp.logical_not(there(against(DIRS[k]))))
            def _():
                buf[at] = jnp.zeros(buf.shape[1:], jnp.float32)

    def scale_rows(row, count):
        def step(i):
            for half in range(2):
                u0[RAD + row + i, half, YO : YO + N[0]] = u0[RAD + row + i, half, YO : YO + N[0]] * sd[row + i, half]

        loop(count, step, 2)

    for copy in loads[:8]:
        copy.wait()
    scale_rows(0, 8)
    scale_rows(40, 8)
    near_x = 3 - west.astype(jnp.int32) - east.astype(jnp.int32)
    near_y = 3 - south.astype(jnp.int32) - north.astype(jnp.int32)
    pl.semaphore_wait(barrier, near_x * near_y - 1)
    start(gather_copy, 0, (0, 1, 4, 5, 6, 7))
    for copy in loads[8:12]:
        copy.wait()
    scale_rows(8, 32)
    start(gather_copy, 0, (2, 3))

    block = slice(YO, YO + N[0])
    restrict_rows(u0, RAD, N[0], block, x1, 28, 7, block)
    restrict_cols(x1, 1, c1, 28, 32)
    clear_edges(c1, 2, 24, 2, 28, True)
    start(scatter_copy, 1)
    restrict_rows(c1, 0, 28, slice(0, 32), x2, 18, 7, slice(8, 40))
    restrict_cols(x2, 1, c2, 18, 24)
    clear_edges(c2, 3, 12, 3, 18, True)
    start(scatter_copy, 2)
    restrict_rows(c2, 0, 18, slice(0, 24), x3, 12, 6, slice(8, 32))
    restrict_cols(x3, 2, c3, 12, 16)
    start(scatter_copy, 3)

    loads[12].wait()
    loads[13].wait()
    for gen in range(GENS):

        def split(i, gen=gen):
            rows = pl.ds(pl.multiple_of(i * 64, 64), 64)
            scaled = mats[gen, rows, :] * gains[gen : gen + 1, :]
            high = scaled.astype(jnp.bfloat16)
            low = (scaled - high.astype(jnp.float32)).astype(jnp.bfloat16)
            weights[gen, pl.ds(pl.multiple_of(i * 64, 64), 64), :] = high
            weights[gen, pl.ds(pl.multiple_of(i * 64 + 256, 64), 64), :] = low
            weights[gen, pl.ds(pl.multiple_of(i * 64 + 512, 64), 64), :] = high

        loop(4, split)
    arrive(gather_copy, 0)
    filter_cols(u0, YO - RAD, y0, 54, N[0])
    filter_rows(y0, d0, N[0])

    def add_up(gen):
        n, e, rim, buf, own = N[gen], OUT[gen], RIM[gen], ext[gen], (c1, c2, c3)[gen - 1]
        rx, ry, rc = ((rx1, ry1, rc1), (rx2, ry2, rc2), (rx3, ry3, rc3))[gen - 1]
        low, high = slice(YO, YO + e), slice(YO + n - e, YO + n)
        inner = slice(YO, YO + n)

        def step(i):
            for half in range(2):
                buf[rim + i, half, inner] = own[e + i, half, e : e + n]
                buf[rim + i, half, low] = buf[rim + i, half, low] + ry[0, i, half, 0:e]
                buf[rim + i, half, high] = buf[rim + i, half, high] + ry[1, i, half, 0:e]

        loop(n, step, 2)
        for i in range(e):
            for half in range(2):
                for side, row in ((0, rim + i), (1, rim + n - e + i)):
                    buf[row, half, inner] = buf[row, half, inner] + rx[side, i, half, 0:n]
                    buf[row, half, low] = buf[row, half, low] + rc[2 * side, i, half, 0:e]
                    buf[row, half, high] = buf[row, half, high] + rc[2 * side + 1, i, half, 0:e]

    for gen in (3, 2, 1):
        arrive(scatter_copy, gen)
        add_up(gen)
        start(gather_copy, gen)

    mix(d0, weights, 0, 4, 12, N[0], 2)

    arrive(gather_copy, 3)
    filter_cols(u3, YO - 6, y3, 18, 16)
    filter_rows(y3, d3, 12)
    mix(d3, weights, 3, 12, 1, 16, 1)
    clear_edges(d3, 3, 6, 3, 12, True)
    prolong_cols(d3, t3, 12, 12, True)
    arrive(gather_copy, 2)
    filter_cols(u2, YO - 6, y2, 24, 24)
    filter_rows(y2, d2, 18)
    mix(d2, weights, 2, 9, 2, 24, 1)

    def add_2(m):
        for half in range(2):
            first, second = prolong_rows(t3, m, half, True)
            d2[2 * m, half] = d2[2 * m, half] + first
            d2[2 * m + 1, half] = d2[2 * m + 1, half] + second

    loop(9, add_2)
    clear_edges(d2, 3, 12, 3, 18, True)
    prolong_cols(d2, t2, 18, 16, False)
    arrive(gather_copy, 1)
    filter_cols(u1, YO - 5, y1, 34, 32)
    filter_rows(y1, d1, 28)
    mix(d1, weights, 1, 4, 7, 32, 1)

    def add_1(m):
        for half in range(2):
            first, second = prolong_rows(t2, m, half, False)
            d1[2 * m, half] = d1[2 * m, half] + first
            d1[2 * m + 1, half] = d1[2 * m + 1, half] + second

    loop(14, add_1)
    clear_edges(d1, 2, 24, 2, 28, True)
    prolong_cols(d1, t1, 28, 24, False)

    def finish(m):
        for half in range(2):
            lanes = slice(half * LANE, (half + 1) * LANE)
            first, second = prolong_rows(t1, m, half, False)
            out[2 * m, :, lanes] = (d0[2 * m, half] + first) * sd[2 * m, half]
            out[2 * m + 1, :, lanes] = (d0[2 * m + 1, half] + second) * sd[2 * m + 1, half]

    loop(24, finish, 2)
    for gen in range(GENS):
        sent(gather_copy, gen)
    for gen in range(1, GENS):
        sent(scatter_copy, gen)


def solution(mesh):
    size_x, size_y = mesh.shape["gx"], mesh.shape["gy"]

    def body(field, stdev, mixing, gen_weight):
        def vmem(*shape, dtype=jnp.float32):
            return pltpu.VMEM(shape, dtype)

        def planes(x, y):
            return vmem(x, 2, y, LANE)

        return pl.pallas_call(
            functools.partial(kernel, size_x, size_y),
            out_shape=jax.ShapeDtypeStruct(field.shape, jnp.float32),
            in_specs=[pl.BlockSpec(memory_space=pltpu.HBM)] * 4,
            out_specs=pl.BlockSpec(memory_space=pltpu.VMEM),
            scratch_shapes=[
                planes(54, 64), planes(34, 48), planes(24, 32), planes(18, 24),
                planes(48, 48), vmem(4, 256, 256), vmem(4, 256), vmem(4, 768, 256, dtype=jnp.bfloat16),
                planes(28, 72), planes(18, 56), planes(12, 40),
                planes(28, 32), planes(18, 24), planes(12, 16),
                vmem(2, 2, 2, 24, LANE), vmem(2, 3, 2, 16, LANE), vmem(2, 3, 2, 8, LANE),
                vmem(2, 24, 2, 8, LANE), vmem(2, 12, 2, 8, LANE), vmem(2, 6, 2, 8, LANE),
                vmem(4, 2, 2, 8, LANE), vmem(4, 3, 2, 8, LANE), vmem(4, 3, 2, 8, LANE),
                planes(54, 48), planes(34, 32), planes(24, 24), planes(18, 16),
                planes(48, 48), planes(28, 32), planes(18, 24), planes(12, 16),
                planes(28, 48), planes(18, 32), planes(12, 24),
                pltpu.SemaphoreType.DMA((14,)),
                pltpu.SemaphoreType.DMA((56,)),
                pltpu.SemaphoreType.DMA((56,)),
            ],
            compiler_params=pltpu.CompilerParams(
                collective_id=0, has_side_effects=True, vmem_limit_bytes=44 * 2**20
            ),
            cost_estimate=pl.CostEstimate(flops=2 * 3556 * 768 * 256, bytes_accessed=8 * 2**20, transcendentals=0),
            name="multigrid",
        )(field, stdev, mixing, gen_weight)

    return jax.shard_map(
        body,
        mesh=mesh,
        in_specs=(P("gx", "gy", None), P("gx", "gy", None), P(), P()),
        out_specs=P("gx", "gy", None),
        check_vma=False,
    )
```

profile of v0, /device:TPU:121, one launch (start us, length us, event | category | flops | bytes accessed | tf_op | source)
XLA Modules:
  0.0 37.7 jit_solution(3020939736318213433)
XLA Ops:
  0.0 0.0 copy-start
  0.0 1.7 %copy-done = f32[48,48,256]{2,1,0:T(8,128)S(1)} copy-done((f32[48,48,256]{2,1,0:T(8,128)S(1)}, f32[48,48,256]{2,1,0:T(8,128)}, u32[]{:S(2)}) %copy-start) | copy-done | bytes 2359320
  1.7 0.0 copy-start.1
  1.7 1.7 %copy-done.1 = f32[48,48,256]{2,1,0:T(8,128)S(1)} copy-done((f32[48,48,256]{2,1,0:T(8,128)S(1)}, f32[48,48,256]{2,1,0:T(8,128)}, u32[]{:S(2)}) %copy-start.1) | copy-done | bytes 2359320
  3.3 0.0 copy-start.2
  3.3 1.2 %copy-done.2 = f32[4,256,256]{2,1,0:T(8,128)S(1)} copy-done((f32[4,256,256]{2,1,0:T(8,128)S(1)}, f32[4,256,256]{2,1,0:T(8,128)}, u32[]{:S(2)}) %copy-start.2) | copy-done | bytes 1048600
  4.6 0.0 copy-start.3
  4.6 0.7 %copy-done.3 = f32[4,256]{1,0:T(4,128)S(1)} copy-done((f32[4,256]{1,0:T(4,128)S(1)}, f32[4,256]{1,0:T(4,128)}, u32[]{:S(2)}) %copy-start.3) | copy-done | bytes 4120
  5.2 31.1 %multigrid.1 = f32[48,48,256]{2,1,0:T(8,128)S(1)} custom-call(f32[48,48,256]{2,1,0:T(8,128)S(1)} %copy-done, f32[48,48,256]{2,1,0:T(8,128)S(1)} %copy-done.1, f32[4,256,256]{2,1,0:T(8,128)S(1)} %copy-done.2, f32[4,256]{1,0:T(4,128)S(1)} %copy-done.3), custom_call_target="tpu_custom_call" | custom-call | flops 1398276096 | bytes 8388608 | tf_op jit(solution)/shard_map/multigrid/pallas_call | solution.py:405
  36.3 1.4 %copy.6 = f32[48,48,256]{2,1,0:T(8,128)} copy(f32[48,48,256]{2,1,0:T(8,128)S(1)} %multigrid.1) | data formatting | bytes 4718592
Async XLA Ops:
  0.0 1.7 %copy-start = (f32[48,48,256]{2,1,0:T(8,128)S(1)}, f32[48,48,256]{2,1,0:T(8,128)}, u32[]{:S(2)}) copy-start(f32[48,48,256]{2,1,0:T(8,128)} %field.1) | copy-start | bytes 7077892
  1.7 1.7 %copy-start.1 = (f32[48,48,256]{2,1,0:T(8,128)S(1)}, f32[48,48,256]{2,1,0:T(8,128)}, u32[]{:S(2)}) copy-start(f32[48,48,256]{2,1,0:T(8,128)} %stdev.1) | copy-start | bytes 7077892
  3.3 1.2 %copy-start.2 = (f32[4,256,256]{2,1,0:T(8,128)S(1)}, f32[4,256,256]{2,1,0:T(8,128)}, u32[]{:S(2)}) copy-start(f32[4,256,256]{2,1,0:T(8,128)} %mixing.1) | copy-start | bytes 3145732
  4.6 0.7 %copy-start.3 = (f32[4,256]{1,0:T(4,128)S(1)}, f32[4,256]{1,0:T(4,128)}, u32[]{:S(2)}) copy-start(f32[4,256]{1,0:T(4,128)} %gen_weight.1) | copy-start | bytes 12292
where the time goes:
time: 38 us; the launch traced here: 37.7 us
  Pallas kernels  31.1 us (82%)
  local copies, waits for them, and re-layouts  6.65 us (18%)
    pallas_call x1, Pallas kernels, body(): pl.pallas_call(functools.partial(kernel, size_x, size_y), out_shape=jax.S...  31.1 us
    unnamed x9, local copies, waits for them, and re-layouts  6.65 us

commit v1 on v0

v1 whole, which is shorter than its diff:
```python
import functools

import jax
import jax.numpy as jnp
from jax import lax
from jax.experimental import pallas as pl
from jax.experimental.pallas import tpu as pltpu
from jax.sharding import PartitionSpec as P

RAD = 3
GENS = 4
LANE = 128
MESH = pl.DeviceIdType.MESH
DIRS = [(1, 0), (-1, 0), (0, 1), (0, -1), (1, 1), (1, -1), (-1, 1), (-1, -1)]
N = (48, 24, 12, 6)
RIM = (3, 5, 6, 6)
OUT = (0, 2, 3, 3)
YO = 8

_total = sum((1.0 - (k / (RAD + 1.0)) ** 2) ** 2 for k in range(-RAD, RAD + 1))
B = [(1.0 - (k / (RAD + 1.0)) ** 2) ** 2 / _total for k in range(RAD + 1)]
DOWN = [B[3], B[2] + B[3], B[1] + B[2], B[0] + B[1], B[0] + B[1], B[1] + B[2], B[2] + B[3], B[3]]
EVEN = [B[3], B[1] + B[2], B[0] + B[1], B[2] + B[3]]
ODD = EVEN[::-1]


def loop(count, step, unroll=1):
    def one(i, carry):
        step(i)
        return carry

    lax.fori_loop(0, count, one, 0, unroll=unroll)


def filtered(load):
    return load(3) * B[0] + (load(2) + load(4)) * B[1] + (load(1) + load(5)) * B[2] + (load(0) + load(6)) * B[3]


def restricted(load):
    return (
        (load(3) + load(4)) * DOWN[3]
        + (load(2) + load(5)) * DOWN[2]
        + (load(1) + load(6)) * DOWN[1]
        + (load(0) + load(7)) * DOWN[0]
    )


def dotted(weights, parts, scale=1.0):
    total = parts[0] * (weights[0] * scale)
    for weight, part in zip(weights[1:], parts[1:]):
        total = total + part * (weight * scale)
    return total


def restrict_rows(src, first, count, dst, span, shift, cols, dst_first):
    whole = [i for i in span if 2 * i - shift >= 0 and 2 * i - shift + 7 < count]
    low, high = whole[0], whole[-1] + 1
    dst_cols = slice(dst_first, dst_first + cols)
    for half in range(2):
        for i in [i for i in span if i not in whole]:
            taps = [t for t in range(8) if 0 <= 2 * i - shift + t < count]
            parts = [src[first + 2 * i - shift + t, half, 0:cols] for t in taps]
            dst[i, half, dst_cols] = dotted([DOWN[t] for t in taps], parts, 0.5)

    def step(j):
        for half in range(2):
            base = first + 2 * (j + low) - shift
            dst[j + low, half, dst_cols] = restricted(lambda t: src[base + t, half, 0:cols]) * 0.5

    loop(high - low, step, 4)


def restrict_cols(src, start, dst, rows, cols):
    def step(i):
        for half in range(2):
            dst[i, half] = restricted(lambda t: src[i, half, pl.ds(start + t, cols, stride=2)])

    loop(rows, step, 2)


def filter_cols(src, start, dst, rows, cols):
    def step(i):
        for half in range(2):
            dst[i, half] = filtered(lambda t: src[i, half, pl.ds(start + t, cols)])

    loop(rows, step, 2)


def filter_rows(src, dst, rows, cols):
    def step(i):
        for half in range(2):
            dst[i, half, YO : YO + cols] = filtered(lambda t: src[i + t, half, 0:cols])

    loop(rows, step, 2)


def prolong_cols(src, dst, rows, count, odd_first):
    def step(i):
        for half in range(2):
            parts = [src[i, half, pl.ds(t, count)] for t in range(4 if odd_first else 5)]
            if odd_first:
                lead, next_one = dotted(ODD, parts), dotted(EVEN, parts)
            else:
                lead, next_one = dotted(EVEN, parts[:4]), dotted(ODD, parts[1:])
            dst[i, half, pl.ds(0, count, stride=2)] = lead
            dst[i, half, pl.ds(1, count, stride=2)] = next_one

    loop(rows, step, 2)


def prolong_rows(src, m, half, odd_first):
    parts = [src[m + t, half] for t in range(4 if odd_first else 5)]
    if odd_first:
        return dotted(ODD, parts, 0.5), dotted(EVEN, parts, 0.5)
    return dotted(EVEN, parts[:4], 0.5), dotted(ODD, parts[1:], 0.5)


def mix(src, dst, weights, gen, first, rows_each, steps, cols):
    count = rows_each * cols

    def step(i):
        rows = pl.ds(first + i * rows_each, rows_each)
        cells = jnp.concatenate([src[rows, half].reshape(count, LANE) for half in range(2)], axis=1)
        high = cells.astype(jnp.bfloat16)
        low = (cells - high.astype(jnp.float32)).astype(jnp.bfloat16)
        product = jnp.dot(
            jnp.concatenate([high, high, low], axis=1), weights[gen], preferred_element_type=jnp.float32
        )
        for half in range(2):
            dst[rows, half] = product[:, half * LANE : (half + 1) * LANE].reshape(rows_each, cols, LANE)

    loop(steps, step)


def kernel(
    size_x, size_y, field, stdev, mixing, gen_weight, out,
    u0, u1, u2, u3, sd, mats, gains, weights,
    x1, x2, x3, c1, c2, c3,
    rx1, rx2, rx3, ry1, ry2, ry3, rc1, rc2, rc3,
    w0, w1, w2, w3, k0, k1, k2, k3, d0, d1, d2, d3, t1, t2, t3,
    load_sem, send_sem, recv_sem,
):
    gx, gy = lax.axis_index("gx"), lax.axis_index("gy")
    west, east = gx == 0, gx == size_x - 1
    south, north = gy == 0, gy == size_y - 1
    wide, tall = (u0, u1, u2, u3), (w0, w1, w2, w3)
    landings = ((rx1, ry1, rc1), (rx2, ry2, rc2), (rx3, ry3, rc3))

    def there(d):
        nx, ny = gx + d[0], gy + d[1]
        return (nx >= 0) & (nx < size_x) & (ny >= 0) & (ny < size_y)

    def against(d):
        return (-d[0], -d[1])

    loads = []
    for row, count in ((0, 8), (40, 8), (8, 16), (24, 16)):
        for half in range(2):
            lanes, rows = pl.ds(half * LANE, LANE), pl.ds(row, count)
            for src, dst in ((field, u0.at[pl.ds(row + RAD, count), half]), (stdev, sd.at[rows, half])):
                loads.append(pltpu.make_async_copy(src.at[rows, :, lanes], dst, load_sem.at[len(loads)]))
    for src, dst in ((mixing, mats), (gen_weight, gains)):
        loads.append(pltpu.make_async_copy(src, dst, load_sem.at[len(loads)]))
    for copy in loads:
        copy.start()

    barrier = pltpu.get_barrier_semaphore()
    for d in DIRS:

        @pl.when(there(d))
        def _():
            pl.semaphore_signal(barrier, inc=1, device_id=(gx + d[0], gy + d[1]), device_id_type=MESH)

    def remote(src, dst, slot, d):
        return pltpu.make_async_remote_copy(
            src_ref=src, dst_ref=dst, send_sem=send_sem.at[slot], recv_sem=recv_sem.at[slot],
            device_id=(gx + d[0], gy + d[1]), device_id_type=MESH,
        )

    def rim_span(step, first, n, rim):
        if step > 0:
            return pl.ds(first + n - rim, rim), pl.ds(first - rim, rim)
        return pl.ds(first, rim), pl.ds(first + n, rim)

    def gather_x(gen, k):
        n, rim, buf = N[gen], RIM[gen], wide[gen]
        src, dst = rim_span(DIRS[k][0], rim, n, rim)
        return remote(buf.at[src, :, pl.ds(0, n)], buf.at[dst, :, pl.ds(0, n)], gen * 2 + k, DIRS[k])

    def gather_y(gen, k):
        n, rim, buf = N[gen], RIM[gen], tall[gen]
        src, dst = rim_span(DIRS[k][1], YO, n, rim)
        return remote(buf.at[:, :, src], buf.at[:, :, dst], 8 + gen * 2 + k - 2, DIRS[k])

    def scatter(gen, k):
        d, n, e, buf = DIRS[k], N[gen], OUT[gen], (c1, c2, c3)[gen - 1]
        rx, ry, rc = landings[gen - 1]
        if k < 2:
            dst = rx.at[k, :, :, pl.ds(0, n)]
        elif k < 4:
            dst = ry.at[k - 2, :, :, pl.ds(0, e)]
        else:
            dst = rc.at[k - 4, :, :, pl.ds(0, e)]

        def span(step):
            return pl.ds(e, n) if step == 0 else pl.ds(n + e, e) if step > 0 else pl.ds(0, e)

        return remote(buf.at[span(d[0]), :, span(d[1])], dst, 16 + (gen - 1) * 8 + k, d)

    ways = {gather_x: (0, 1), gather_y: (2, 3), scatter: (4, 5, 6, 7, 0, 1, 2, 3)}
    open_sends, open_receives = [], []

    def start(make, gen):
        open_sends.append((make, gen))
        open_receives.append((make, gen))
        for k in ways[make]:
            pl.when(there(DIRS[k]))(lambda k=k: make(gen, k).start())

    def arrive(make, gen):
        open_receives.remove((make, gen))
        for k in ways[make]:
            pl.when(there(against(DIRS[k])))(lambda k=k: make(gen, k).wait_recv())

    def sent(make, gen):
        for k in ways[make]:
            pl.when(there(DIRS[k]))(lambda k=k: make(gen, k).wait_send())

    def clear_cols(buf, rows, first, count):
        def step(i):
            buf[i, :, first : first + count] = jnp.zeros((2, count, LANE), jnp.float32)

        loop(rows, step, 2)

    def clear_rows(buf, first, count):
        for i in range(count):
            buf[first + i] = jnp.zeros(buf.shape[1:], jnp.float32)

    def clear_edges(buf, width, n):
        pl.when(west)(lambda: clear_rows(buf, 0, width))
        pl.when(east)(lambda: clear_rows(buf, width + n, width))
        pl.when(south)(lambda: clear_cols(buf, n + 2 * width, 0, width))
        pl.when(north)(lambda: clear_cols(buf, n + 2 * width, width + n, width))

    clear_cols(x1, 28, 0, 8)
    clear_cols(x1, 28, 56, 16)
    clear_cols(x2, 18, 0, 8)
    clear_cols(x2, 18, 40, 16)
    clear_cols(x3, 12, 0, 8)
    clear_cols(x3, 12, 32, 8)
    for gen in range(GENS):
        n, rim, rows = N[gen], RIM[gen], N[gen] + 2 * OUT[gen]
        pl.when(west)(lambda: clear_rows(wide[gen], 0, rim))
        pl.when(east)(lambda: clear_rows(wide[gen], rim + n, rim))
        pl.when(south)(lambda: clear_cols(tall[gen], rows, YO - rim, rim))
        pl.when(north)(lambda: clear_cols(tall[gen], rows, YO + n, rim))
    for gen in range(1, GENS):
        rx, ry, rc = landings[gen - 1]
        for k in range(8):
            buf, at = (rx, k) if k < 2 else (ry, k - 2) if k < 4 else (rc, k - 4)

            @pl.when(jnp.logical_not(there(against(DIRS[k]))))
            def _():
                buf[at] = jnp.zeros(buf.shape[1:], jnp.float32)

    def scale_rows(row, count):
        def step(i):
            for half in range(2):
                u0[RAD + row + i, half] = u0[RAD + row + i, half] * sd[row + i, half]

        loop(count, step, 2)

    for copy in loads[:8]:
        copy.wait()
    scale_rows(0, 8)
    scale_rows(40, 8)
    near_x = 3 - west.astype(jnp.int32) - east.astype(jnp.int32)
    near_y = 3 - south.astype(jnp.int32) - north.astype(jnp.int32)
    pl.semaphore_wait(barrier, near_x * near_y - 1)
    start(gather_x, 0)
    for copy in loads[8:12]:
        copy.wait()
    scale_rows(8, 16)
    restrict_rows(u0, RAD, N[0], x1, range(0, 12), 7, N[0], YO)
    for copy in loads[12:16]:
        copy.wait()
    scale_rows(24, 16)
    restrict_rows(u0, RAD, N[0], x1, range(12, 28), 7, N[0], YO)
    restrict_cols(x1, 1, c1, 28, 32)
    clear_edges(c1, 2, 24)
    start(scatter, 1)
    restrict_rows(c1, 0, 28, x2, range(18), 7, 32, 8)
    restrict_cols(x2, 1, c2, 18, 24)
    clear_edges(c2, 3, 12)
    start(scatter, 2)
    restrict_rows(c2, 0, 18, x3, range(12), 6, 24, 8)
    restrict_cols(x3, 2, c3, 12, 16)
    start(scatter, 3)
    for copy in loads[16:]:
        copy.wait()
    for gen in range(GENS):

        def split(i, gen=gen):
            scaled = mats[gen, pl.ds(pl.multiple_of(i * 64, 64), 64), :] * gains[gen : gen + 1, :]
            high = scaled.astype(jnp.bfloat16)
            low = (scaled - high.astype(jnp.float32)).astype(jnp.bfloat16)
            for place, part in ((0, high), (256, low), (512, high)):
                weights[gen, pl.ds(pl.multiple_of(i * 64 + place, 64), 64), :] = part

        loop(4, split)
    arrive(gather_x, 0)
    filter_rows(u0, w0, N[0], N[0])
    start(gather_y, 0)
    def add_up(gen):
        n, e, rim, buf, own = N[gen], OUT[gen], RIM[gen], wide[gen], (c1, c2, c3)[gen - 1]
        rx, ry, rc = landings[gen - 1]
        low, high = slice(0, e), slice(n - e, n)

        def step(i):
            for half in range(2):
                buf[rim + i, half, 0:n] = own[e + i, half, e : e + n]
                buf[rim + i, half, low] = buf[rim + i, half, low] + ry[0, i, half, 0:e]
                buf[rim + i, half, high] = buf[rim + i, half, high] + ry[1, i, half, 0:e]

        loop(n, step, 2)
        for i in range(e):
            for half in range(2):
                for side, row in ((0, rim + i), (1, rim + n - e + i)):
                    buf[row, half, 0:n] = buf[row, half, 0:n] + rx[side, i, half, 0:n]
                    buf[row, half, low] = buf[row, half, low] + rc[2 * side, i, half, 0:e]
                    buf[row, half, high] = buf[row, half, high] + rc[2 * side + 1, i, half, 0:e]

    for gen in (1, 2, 3):
        arrive(scatter, gen)
        add_up(gen)
        start(gather_x, gen)
    arrive(gather_y, 0)
    filter_cols(w0, YO - RAD, k0, N[0], N[0])
    mix(k0, d0, weights, 0, 0, 8, 3, N[0])
    for gen in (1, 2, 3):
        arrive(gather_x, gen)
        filter_rows(wide[gen], tall[gen], N[gen] + 2 * OUT[gen], N[gen])
        start(gather_y, gen)
    mix(k0, d0, weights, 0, 24, 8, 3, N[0])
    arrive(gather_y, 1)
    filter_cols(w1, YO - 5, k1, 28, 32)
    mix(k1, d1, weights, 1, 0, 14, 2, 32)
    arrive(gather_y, 2)
    filter_cols(w2, YO - 6, k2, 18, 24)
    mix(k2, d2, weights, 2, 0, 18, 1, 24)
    arrive(gather_y, 3)
    filter_cols(w3, YO - 6, k3, 12, 16)
    mix(k3, d3, weights, 3, 0, 12, 1, 16)
    clear_edges(d3, 3, 6)
    prolong_cols(d3, t3, 12, 12, True)

    def add_2(m):
        for half in range(2):
            first, second = prolong_rows(t3, m, half, True)
            d2[2 * m, half] = d2[2 * m, half] + first
            d2[2 * m + 1, half] = d2[2 * m + 1, half] + second

    loop(9, add_2, 3)
    clear_edges(d2, 3, 12)
    prolong_cols(d2, t2, 18, 16, False)

    def add_1(m):
        for half in range(2):
            first, second = prolong_rows(t2, m, half, False)
            d1[2 * m, half] = d1[2 * m, half] + first
            d1[2 * m + 1, half] = d1[2 * m + 1, half] + second

    loop(14, add_1, 2)
    clear_edges(d1, 2, 24)
    prolong_cols(d1, t1, 28, 24, False)

    def finish(m):
        for half in range(2):
            lanes = slice(half * LANE, (half + 1) * LANE)
            first, second = prolong_rows(t1, m, half, False)
            out[2 * m, :, lanes] = (d0[2 * m, half] + first) * sd[2 * m, half]
            out[2 * m + 1, :, lanes] = (d0[2 * m + 1, half] + second) * sd[2 * m + 1, half]

    loop(24, finish, 2)
    for make, gen in list(open_receives):
        arrive(make, gen)
    for make, gen in open_sends:
        sent(make, gen)


def solution(mesh):
    size_x, size_y = mesh.shape["gx"], mesh.shape["gy"]

    def body(field, stdev, mixing, gen_weight):
        def vmem(*shape, dtype=jnp.float32):
            return pltpu.VMEM(shape, dtype)

        def planes(x, y):
            return vmem(x, 2, y, LANE)

        return pl.pallas_call(
            functools.partial(kernel, size_x, size_y),
            out_shape=pltpu.VMEM(field.shape, jnp.float32),
            in_specs=[pl.BlockSpec(memory_space=pl.ANY)] * 4,
            out_specs=pl.BlockSpec(memory_space=pltpu.VMEM),
            scratch_shapes=[
                planes(54, 48), planes(34, 24), planes(24, 16), planes(18, 8),
                planes(48, 48), vmem(4, 256, 256), vmem(4, 256), vmem(4, 768, 256, dtype=jnp.bfloat16),
                planes(28, 72), planes(18, 56), planes(12, 40),
                planes(28, 32), planes(18, 24), planes(12, 16),
                vmem(2, 2, 2, 24, LANE), vmem(2, 3, 2, 16, LANE), vmem(2, 3, 2, 8, LANE),
                vmem(2, 24, 2, 8, LANE), vmem(2, 12, 2, 8, LANE), vmem(2, 6, 2, 8, LANE),
                vmem(4, 2, 2, 8, LANE), vmem(4, 3, 2, 8, LANE), vmem(4, 3, 2, 8, LANE),
                planes(48, 64), planes(28, 48), planes(18, 32), planes(12, 24),
                planes(48, 48), planes(28, 32), planes(18, 24), planes(12, 16),
                planes(48, 48), planes(28, 32), planes(18, 24), planes(12, 16),
                planes(28, 48), planes(18, 32), planes(12, 24),
                pltpu.SemaphoreType.DMA((18,)),
                pltpu.SemaphoreType.DMA((40,)),
                pltpu.SemaphoreType.DMA((40,)),
            ],
            compiler_params=pltpu.CompilerParams(
                collective_id=0, has_side_effects=True, vmem_limit_bytes=44 * 2**20
            ),
            cost_estimate=pl.CostEstimate(flops=2 * 3556 * 768 * 256, bytes_accessed=8 * 2**20, transcendentals=0),
            name="multigrid",
        )(*[pltpu.with_memory_space_constraint(a, pltpu.HBM) for a in (field, stdev, mixing, gen_weight)])

    return jax.shard_map(
        body,
        mesh=mesh,
        in_specs=(P("gx", "gy", None), P("gx", "gy", None), P(), P()),
        out_specs=P("gx", "gy", None),
        check_vma=False,
    )
```

time: 38 us -> 31.1 us (0.82)
  local copies, waits for them, and re-layouts: 6.65 us -> 1.41 us
  Pallas kernels: 31.1 us -> 29.6 us
    unnamed x9 -> x1, local copies, waits for them, and re-layouts: 6.65 us -> 1.41 us
    pallas_call x1, Pallas kernels: 31.1 us -> 29.6 us  [body(): pl.pallas_call(functools.partial(kernel, size_x, size_y), out_shape=pltpu...]
where the time goes in v1:
time: 31.1 us; the launch traced here: 31 us
  Pallas kernels  29.6 us (95%)
  local copies, waits for them, and re-layouts  1.41 us (5%)
    pallas_call x1, Pallas kernels, body(): pl.pallas_call(functools.partial(kernel, size_x, size_y), out_shape=pltpu...  29.6 us
    unnamed x1, local copies, waits for them, and re-layouts  1.41 us

profile of v1, /device:TPU:121, one launch (start us, length us, event | category | flops | bytes accessed | tf_op | source)
XLA Modules:
  0.0 31.0 jit_solution(10950725737814809763)
XLA Ops:
  0.0 29.6 %multigrid.1 = f32[48,48,256]{2,1,0:T(8,128)S(1)} custom-call(f32[48,48,256]{2,1,0:T(8,128)} %field.1, f32[48,48,256]{2,1,0:T(8,128)} %stdev.1, f32[4,256,256]{2,1,0:T(8,128)} %mixing.1, f32[4,256]{1,0:T(4,128)} %gen_weight.1), custom_call_target="tpu_custom_call" | custom-call | flops 1398276096 | bytes 8388608 | tf_op jit(solution)/shard_map/multigrid/pallas_call | solution.py:400
  29.6 1.4 %copy.6 = f32[48,48,256]{2,1,0:T(8,128)} copy(f32[48,48,256]{2,1,0:T(8,128)S(1)} %multigrid.1) | data formatting | bytes 4718592

commit v2 on v1

--- a/solution.py
+++ b/solution.py
@@ -52,20 +52,20 @@
     return total
 
 
-def restrict_rows(src, first, count, dst, span, shift, cols, dst_first):
+def restrict_rows(src, first, count, dst, span, shift, cols, dst_first, src_first=0):
     whole = [i for i in span if 2 * i - shift >= 0 and 2 * i - shift + 7 < count]
     low, high = whole[0], whole[-1] + 1
-    dst_cols = slice(dst_first, dst_first + cols)
+    src_cols, dst_cols = slice(src_first, src_first + cols), slice(dst_first, dst_first + cols)
     for half in range(2):
         for i in [i for i in span if i not in whole]:
             taps = [t for t in range(8) if 0 <= 2 * i - shift + t < count]
-            parts = [src[first + 2 * i - shift + t, half, 0:cols] for t in taps]
+            parts = [src[first + 2 * i - shift + t, half, src_cols] for t in taps]
             dst[i, half, dst_cols] = dotted([DOWN[t] for t in taps], parts, 0.5)
 
     def step(j):
         for half in range(2):
             base = first + 2 * (j + low) - shift
-            dst[j + low, half, dst_cols] = restricted(lambda t: src[base + t, half, 0:cols]) * 0.5
+            dst[j + low, half, dst_cols] = restricted(lambda t: src[base + t, half, src_cols]) * 0.5
 
     loop(high - low, step, 4)
 
@@ -78,24 +78,27 @@
     loop(rows, step, 2)
 
 
-def filter_cols(src, start, dst, rows, cols):
-    def step(i):
+def filter_cols(src, start, dst, rows, cols, first=0):
+    def step(j):
+        i = first + j
         for half in range(2):
             dst[i, half] = filtered(lambda t: src[i, half, pl.ds(start + t, cols)])
 
     loop(rows, step, 2)
 
 
-def filter_rows(src, dst, rows, cols):
-    def step(i):
-        for half in range(2):
-            dst[i, half, YO : YO + cols] = filtered(lambda t: src[i + t, half, 0:cols])
+def filter_rows(src, dst, rows, first=0):
+    def step(j):
+        i = first + j
+        for half in range(2):
+            dst[i, half] = filtered(lambda t: src[i + t, half])
 
     loop(rows, step, 2)
 
 
-def prolong_cols(src, dst, rows, count, odd_first):
-    def step(i):
+def prolong_cols(src, dst, rows, count, odd_first, first=0):
+    def step(j):
+        i = first + j
         for half in range(2):
             parts = [src[i, half, pl.ds(t, count)] for t in range(4 if odd_first else 5)]
             if odd_first:
@@ -133,17 +136,17 @@
 
 
 def kernel(
-    size_x, size_y, field, stdev, mixing, gen_weight, out,
-    u0, u1, u2, u3, sd, mats, gains, weights,
+    size_x, size_y, field, stdev, mixing, gen_weight, d0, d1, sd,
+    f0, u0, u1, u2, u3, mats, gains, weights,
     x1, x2, x3, c1, c2, c3,
     rx1, rx2, rx3, ry1, ry2, ry3, rc1, rc2, rc3,
-    w0, w1, w2, w3, k0, k1, k2, k3, d0, d1, d2, d3, t1, t2, t3,
+    y0, y1, y2, y3, k0, k1, k2, k3, d2, d3, t2, t3,
     load_sem, send_sem, recv_sem,
 ):
     gx, gy = lax.axis_index("gx"), lax.axis_index("gy")
     west, east = gx == 0, gx == size_x - 1
     south, north = gy == 0, gy == size_y - 1
-    wide, tall = (u0, u1, u2, u3), (w0, w1, w2, w3)
+    ext = (u0, u1, u2, u3)
     landings = ((rx1, ry1, rc1), (rx2, ry2, rc2), (rx3, ry3, rc3))
 
     def there(d):
@@ -154,14 +157,13 @@
         return (-d[0], -d[1])
 
     loads = []
-    for row, count in ((0, 8), (40, 8), (8, 16), (24, 16)):
-        for half in range(2):
-            lanes, rows = pl.ds(half * LANE, LANE), pl.ds(row, count)
-            for src, dst in ((field, u0.at[pl.ds(row + RAD, count), half]), (stdev, sd.at[rows, half])):
-                loads.append(pltpu.make_async_copy(src.at[rows, :, lanes], dst, load_sem.at[len(loads)]))
+    for row, count in ((0, 24), (24, 24)):
+        rows = pl.ds(row, count)
+        for src, dst in ((field, f0), (stdev, sd)):
+            loads.append(pltpu.make_async_copy(src.at[rows], dst.at[rows], load_sem.at[len(loads)]))
     for src, dst in ((mixing, mats), (gen_weight, gains)):
         loads.append(pltpu.make_async_copy(src, dst, load_sem.at[len(loads)]))
-    for copy in loads:
+    for copy in loads[:4]:
         copy.start()
 
     barrier = pltpu.get_barrier_semaphore()
@@ -183,14 +185,30 @@
         return pl.ds(first, rim), pl.ds(first + n, rim)
 
     def gather_x(gen, k):
-        n, rim, buf = N[gen], RIM[gen], wide[gen]
+        n, rim, buf = N[gen], RIM[gen], ext[gen]
         src, dst = rim_span(DIRS[k][0], rim, n, rim)
-        return remote(buf.at[src, :, pl.ds(0, n)], buf.at[dst, :, pl.ds(0, n)], gen * 2 + k, DIRS[k])
+        cols = pl.ds(YO, n)
+        return remote(buf.at[src, :, cols], buf.at[dst, :, cols], gen * 2 + k, DIRS[k])
 
     def gather_y(gen, k):
-        n, rim, buf = N[gen], RIM[gen], tall[gen]
+        n, rim, buf = N[gen], RIM[gen], ext[gen]
         src, dst = rim_span(DIRS[k][1], YO, n, rim)
-        return remote(buf.at[:, :, src], buf.at[:, :, dst], 8 + gen * 2 + k - 2, DIRS[k])
+        rows = pl.ds(rim, n)
+        return remote(buf.at[rows, :, src], buf.at[rows, :, dst], 8 + gen * 2 + k - 2, DIRS[k])
+
+    def gather_corner(gen, k):
+        n, rim, buf = N[gen], RIM[gen], ext[gen]
+        src, dst = rim_span(DIRS[k % 4][1], YO, n, rim)
+        rows = pl.ds(rim + n if k < 4 else 0, rim)
+        return remote(buf.at[rows, :, src], buf.at[rows, :, dst], 48 + gen * 4 + k % 2 + k // 4 * 2, DIRS[k % 4])
+
+    def gather_0(gen, k):
+        d, n, rim = DIRS[k], N[0], RIM[0]
+        (sx, tx), (sy, ty) = [
+            (pl.ds(first, n), pl.ds(first, n)) if step == 0 else rim_span(step, first, n, rim)
+            for step, first in ((d[0], rim), (d[1], YO))
+        ]
+        return remote(u0.at[sx, :, sy], u0.at[tx, :, ty], 40 + k, d)
 
     def scatter(gen, k):
         d, n, e, buf = DIRS[k], N[gen], OUT[gen], (c1, c2, c3)[gen - 1]
@@ -207,23 +225,39 @@
 
         return remote(buf.at[span(d[0]), :, span(d[1])], dst, 16 + (gen - 1) * 8 + k, d)
 
-    ways = {gather_x: (0, 1), gather_y: (2, 3), scatter: (4, 5, 6, 7, 0, 1, 2, 3)}
+    ways = {
+        gather_x: (0, 1),
+        gather_y: (2, 3),
+        gather_corner: (2, 3, 6, 7),
+        gather_0: (0, 1, 4, 5, 6, 7),
+        scatter: (0, 1, 2, 3, 4, 5, 6, 7),
+    }
     open_sends, open_receives = [], []
+
+    def goes(make, k):
+        if make is gather_corner:
+            return there(DIRS[k % 4]) & there(DIRS[k // 4])
+        return there(DIRS[k])
+
+    def comes(make, k):
+        if make is gather_corner:
+            return there(against(DIRS[k % 4])) & there(DIRS[k // 4])
+        return there(against(DIRS[k]))
 
     def start(make, gen):
         open_sends.append((make, gen))
         open_receives.append((make, gen))
         for k in ways[make]:
-            pl.when(there(DIRS[k]))(lambda k=k: make(gen, k).start())
+            pl.when(goes(make, k))(lambda k=k: make(gen, k).start())
 
     def arrive(make, gen):
         open_receives.remove((make, gen))
         for k in ways[make]:
-            pl.when(there(against(DIRS[k])))(lambda k=k: make(gen, k).wait_recv())
+            pl.when(comes(make, k))(lambda k=k: make(gen, k).wait_recv())
 
     def sent(make, gen):
         for k in ways[make]:
-            pl.when(there(DIRS[k]))(lambda k=k: make(gen, k).wait_send())
+            pl.when(goes(make, k))(lambda k=k: make(gen, k).wait_send())
 
     def clear_cols(buf, rows, first, count):
         def step(i):
@@ -248,11 +282,11 @@
     clear_cols(x3, 12, 0, 8)
     clear_cols(x3, 12, 32, 8)
     for gen in range(GENS):
-        n, rim, rows = N[gen], RIM[gen], N[gen] + 2 * OUT[gen]
-        pl.when(west)(lambda: clear_rows(wide[gen], 0, rim))
-        pl.when(east)(lambda: clear_rows(wide[gen], rim + n, rim))
-        pl.when(south)(lambda: clear_cols(tall[gen], rows, YO - rim, rim))
-        pl.when(north)(lambda: clear_cols(tall[gen], rows, YO + n, rim))
+        n, rim, buf = N[gen], RIM[gen], ext[gen]
+        pl.when(west)(lambda: clear_rows(buf, 0, rim))
+        pl.when(east)(lambda: clear_rows(buf, rim + n, rim))
+        pl.when(south)(lambda: clear_cols(buf, n + 2 * rim, YO - rim, rim))
+        pl.when(north)(lambda: clear_cols(buf, n + 2 * rim, YO + n, rim))
     for gen in range(1, GENS):
         rx, ry, rc = landings[gen - 1]
         for k in range(8):
@@ -265,29 +299,26 @@
     def scale_rows(row, count):
         def step(i):
             for half in range(2):
-                u0[RAD + row + i, half] = u0[RAD + row + i, half] * sd[row + i, half]
+                lanes = slice(half * LANE, (half + 1) * LANE)
+                u0[RAD + row + i, half, YO : YO + N[0]] = f0[row + i, :, lanes] * sd[row + i, :, lanes]
 
         loop(count, step, 2)
 
-    for copy in loads[:8]:
+    for copy in loads[:2]:
         copy.wait()
-    scale_rows(0, 8)
-    scale_rows(40, 8)
+    scale_rows(0, 24)
+    restrict_rows(u0, RAD, N[0], x1, range(0, 12), 7, N[0], YO, YO)
+    for copy in loads[2:4]:
+        copy.wait()
+    for copy in loads[4:]:
+        copy.start()
+    scale_rows(24, 24)
     near_x = 3 - west.astype(jnp.int32) - east.astype(jnp.int32)
     near_y = 3 - south.astype(jnp.int32) - north.astype(jnp.int32)
     pl.semaphore_wait(barrier, near_x * near_y - 1)
-    start(gather_x, 0)
-    for copy in loads[8:12]:
-        copy.wait()
-    scale_rows(8, 16)
-    restrict_rows(u0, RAD, N[0], x1, range(0, 12), 7, N[0], YO)
-    for copy in loads[12:16]:
-        copy.wait()
-    scale_rows(24, 16)
-    restrict_rows(u0, RAD, N[0], x1, range(12, 28), 7, N[0], YO)
+    restrict_rows(u0, RAD, N[0], x1, range(12, 28), 7, N[0], YO, YO)
     restrict_cols(x1, 1, c1, 28, 32)
     clear_edges(c1, 2, 24)
-    start(scatter, 1)
     restrict_rows(c1, 0, 28, x2, range(18), 7, 32, 8)
     restrict_cols(x2, 1, c2, 18, 24)
     clear_edges(c2, 3, 12)
@@ -295,7 +326,9 @@
     restrict_rows(c2, 0, 18, x3, range(12), 6, 24, 8)
     restrict_cols(x3, 2, c3, 12, 16)
     start(scatter, 3)
-    for copy in loads[16:]:
+    start(scatter, 1)
+    start(gather_y, 0)
+    for copy in loads[4:]:
         copy.wait()
     for gen in range(GENS):
 
@@ -307,17 +340,14 @@
                 weights[gen, pl.ds(pl.multiple_of(i * 64 + place, 64), 64), :] = part
 
         loop(4, split)
-    arrive(gather_x, 0)
-    filter_rows(u0, w0, N[0], N[0])
-    start(gather_y, 0)
     def add_up(gen):
-        n, e, rim, buf, own = N[gen], OUT[gen], RIM[gen], wide[gen], (c1, c2, c3)[gen - 1]
+        n, e, rim, buf, own = N[gen], OUT[gen], RIM[gen], ext[gen], (c1, c2, c3)[gen - 1]
         rx, ry, rc = landings[gen - 1]
-        low, high = slice(0, e), slice(n - e, n)
+        inner, low, high = slice(YO, YO + n), slice(YO, YO + e), slice(YO + n - e, YO + n)
 
         def step(i):
             for half in range(2):
-                buf[rim + i, half, 0:n] = own[e + i, half, e : e + n]
+                buf[rim + i, half, inner] = own[e + i, half, e : e + n]
                 buf[rim + i, half, low] = buf[rim + i, half, low] + ry[0, i, half, 0:e]
                 buf[rim + i, half, high] = buf[rim + i, half, high] + ry[1, i, half, 0:e]
 
@@ -325,33 +355,39 @@
         for i in range(e):
             for half in range(2):
                 for side, row in ((0, rim + i), (1, rim + n - e + i)):
-                    buf[row, half, 0:n] = buf[row, half, 0:n] + rx[side, i, half, 0:n]
+                    buf[row, half, inner] = buf[row, half, inner] + rx[side, i, half, 0:n]
                     buf[row, half, low] = buf[row, half, low] + rc[2 * side, i, half, 0:e]
                     buf[row, half, high] = buf[row, half, high] + rc[2 * side + 1, i, half, 0:e]
 
-    for gen in (1, 2, 3):
+    for gen in (3, 2, 1):
         arrive(scatter, gen)
         add_up(gen)
         start(gather_x, gen)
+        start(gather_y, gen)
     arrive(gather_y, 0)
-    filter_cols(w0, YO - RAD, k0, N[0], N[0])
-    mix(k0, d0, weights, 0, 0, 8, 3, N[0])
-    for gen in (1, 2, 3):
+    filter_cols(u0, YO - RAD, y0, N[0], N[0], RAD)
+    filter_rows(y0, k0, 42, RAD)
+    mix(k0, d0, weights, 0, 3, 14, 1, N[0])
+    for gen in (3, 2, 1):
         arrive(gather_x, gen)
-        filter_rows(wide[gen], tall[gen], N[gen] + 2 * OUT[gen], N[gen])
-        start(gather_y, gen)
-    mix(k0, d0, weights, 0, 24, 8, 3, N[0])
-    arrive(gather_y, 1)
-    filter_cols(w1, YO - 5, k1, 28, 32)
-    mix(k1, d1, weights, 1, 0, 14, 2, 32)
-    arrive(gather_y, 2)
-    filter_cols(w2, YO - 6, k2, 18, 24)
-    mix(k2, d2, weights, 2, 0, 18, 1, 24)
-    arrive(gather_y, 3)
-    filter_cols(w3, YO - 6, k3, 12, 16)
+        start(gather_corner, gen)
+        if gen == 2:
+            start(gather_0, 0)
+    for gen in (3, 2, 1):
+        arrive(gather_y, gen)
+    filter_cols(u1, YO - 5, y1, 24, 32, 5)
+    filter_rows(y1, k1, 18, 5)
+    mix(k0, d0, weights, 0, 17, 14, 2, N[0])
+    arrive(gather_corner, 3)
+    filter_cols(u3, YO - 6, y3, 18, 16)
+    filter_rows(y3, k3, 12)
     mix(k3, d3, weights, 3, 0, 12, 1, 16)
     clear_edges(d3, 3, 6)
     prolong_cols(d3, t3, 12, 12, True)
+    arrive(gather_corner, 2)
+    filter_cols(u2, YO - 6, y2, 24, 24)
+    filter_rows(y2, k2, 18)
+    mix(k2, d2, weights, 2, 0, 18, 1, 24)
 
     def add_2(m):
         for half in range(2):
@@ -362,6 +398,12 @@
     loop(9, add_2, 3)
     clear_edges(d2, 3, 12)
     prolong_cols(d2, t2, 18, 16, False)
+    arrive(gather_corner, 1)
+    for first in (0, 29):
+        filter_cols(u1, YO - 5, y1, 5, 32, first)
+    for first in (0, 23):
+        filter_rows(y1, k1, 5, first)
+    mix(k1, d1, weights, 1, 0, 14, 2, 32)
 
     def add_1(m):
         for half in range(2):
@@ -371,22 +413,40 @@
 
     loop(14, add_1, 2)
     clear_edges(d1, 2, 24)
-    prolong_cols(d1, t1, 28, 24, False)
-
-    def finish(m):
-        for half in range(2):
-            lanes = slice(half * LANE, (half + 1) * LANE)
-            first, second = prolong_rows(t1, m, half, False)
-            out[2 * m, :, lanes] = (d0[2 * m, half] + first) * sd[2 * m, half]
-            out[2 * m + 1, :, lanes] = (d0[2 * m + 1, half] + second) * sd[2 * m + 1, half]
-
-    loop(24, finish, 2)
+    arrive(gather_0, 0)
+    filter_cols(u0, YO - RAD, y0, RAD, N[0])
+    filter_cols(u0, YO - RAD, y0, RAD, N[0], N[0] + RAD)
+    for first in (0, N[0] - RAD):
+        filter_rows(y0, k0, RAD, first)
+        mix(k0, d0, weights, 0, first, RAD, 1, N[0])
     for make, gen in list(open_receives):
         arrive(make, gen)
     for make, gen in open_sends:
         sent(make, gen)
 
 
+def finish(d0, d1, sd, out, t1, rows, sems):
+    copies = []
+    for part in range(6):
+        first = 0 if part == 0 else 4 * part + 4
+        prolong_cols(d1, t1, 4 * part + 8 - first, 24, False, first)
+
+        def step(j, part=part):
+            m = 4 * part + j
+            for half in range(2):
+                lanes = slice(half * LANE, (half + 1) * LANE)
+                even, odd = prolong_rows(t1, m, half, False)
+                rows[2 * m, :, lanes] = (d0[2 * m, half] + even) * sd[2 * m, :, lanes]
+                rows[2 * m + 1, :, lanes] = (d0[2 * m + 1, half] + odd) * sd[2 * m + 1, :, lanes]
+
+        loop(4, step, 2)
+        some = pl.ds(8 * part, 8)
+        copies.append(pltpu.make_async_copy(rows.at[some], out.at[some], sems.at[part]))
+        copies[-1].start()
+    for copy in copies:
+        copy.wait()
+
+
 def solution(mesh):
     size_x, size_y = mesh.shape["gx"], mesh.shape["gy"]
 
@@ -397,33 +457,44 @@
         def planes(x, y):
             return vmem(x, 2, y, LANE)
 
-        return pl.pallas_call(
+        inputs = [pltpu.with_memory_space_constraint(a, pltpu.HBM) for a in (field, stdev, mixing, gen_weight)]
+        held = pl.BlockSpec(memory_space=pltpu.VMEM)
+        parts = pl.pallas_call(
             functools.partial(kernel, size_x, size_y),
-            out_shape=pltpu.VMEM(field.shape, jnp.float32),
+            out_shape=(planes(48, 48), planes(28, 32), vmem(*field.shape)),
             in_specs=[pl.BlockSpec(memory_space=pl.ANY)] * 4,
-            out_specs=pl.BlockSpec(memory_space=pltpu.VMEM),
+            out_specs=(held, held, held),
             scratch_shapes=[
-                planes(54, 48), planes(34, 24), planes(24, 16), planes(18, 8),
-                planes(48, 48), vmem(4, 256, 256), vmem(4, 256), vmem(4, 768, 256, dtype=jnp.bfloat16),
+                vmem(*field.shape), planes(54, 64), planes(34, 48), planes(24, 32), planes(18, 24),
+                vmem(4, 256, 256), vmem(4, 256), vmem(4, 768, 256, dtype=jnp.bfloat16),
                 planes(28, 72), planes(18, 56), planes(12, 40),
                 planes(28, 32), planes(18, 24), planes(12, 16),
                 vmem(2, 2, 2, 24, LANE), vmem(2, 3, 2, 16, LANE), vmem(2, 3, 2, 8, LANE),
                 vmem(2, 24, 2, 8, LANE), vmem(2, 12, 2, 8, LANE), vmem(2, 6, 2, 8, LANE),
                 vmem(4, 2, 2, 8, LANE), vmem(4, 3, 2, 8, LANE), vmem(4, 3, 2, 8, LANE),
-                planes(48, 64), planes(28, 48), planes(18, 32), planes(12, 24),
+                planes(54, 48), planes(34, 32), planes(24, 24), planes(18, 16),
                 planes(48, 48), planes(28, 32), planes(18, 24), planes(12, 16),
-                planes(48, 48), planes(28, 32), planes(18, 24), planes(12, 16),
-                planes(28, 48), planes(18, 32), planes(12, 24),
-                pltpu.SemaphoreType.DMA((18,)),
-                pltpu.SemaphoreType.DMA((40,)),
-                pltpu.SemaphoreType.DMA((40,)),
+                planes(18, 24), planes(12, 16),
+                planes(18, 32), planes(12, 24),
+                pltpu.SemaphoreType.DMA((6,)),
+                pltpu.SemaphoreType.DMA((64,)),
+                pltpu.SemaphoreType.DMA((64,)),
             ],
             compiler_params=pltpu.CompilerParams(
-                collective_id=0, has_side_effects=True, vmem_limit_bytes=44 * 2**20
+                collective_id=0, has_side_effects=True, vmem_limit_bytes=40 * 2**20
             ),
             cost_estimate=pl.CostEstimate(flops=2 * 3556 * 768 * 256, bytes_accessed=8 * 2**20, transcendentals=0),
             name="multigrid",
-        )(*[pltpu.with_memory_space_constraint(a, pltpu.HBM) for a in (field, stdev, mixing, gen_weight)])
+        )(*inputs)
+        return pl.pallas_call(
+            finish,
+            out_shape=jax.ShapeDtypeStruct(field.shape, jnp.float32),
+            in_specs=[held] * 3,
+            out_specs=pl.BlockSpec(memory_space=pl.ANY),
+            scratch_shapes=[planes(28, 48), vmem(*field.shape), pltpu.SemaphoreType.DMA((6,))],
+            compiler_params=pltpu.CompilerParams(vmem_limit_bytes=12 * 2**20),
+            name="finish",
+        )(*[pltpu.with_memory_space_constraint(a, pltpu.VMEM) for a in parts])
 
     return jax.shard_map(
         body,

time: 31.1 us -> 28.7 us (0.923)
  local copies, waits for them, and re-layouts: 1.41 us -> 0 us
  Pallas kernels: 29.6 us -> 28.6 us
    unnamed x1 -> x0, local copies, waits for them, and re-layouts: 1.41 us -> none
    pallas_call x1 -> x2, Pallas kernels: 29.6 us -> 28.6 us  [the longest x1 26.6 us: body(): pl.pallas_call(functools.partial(kernel, size_x, size_y), out_shape=(plan...]
where the time goes in v2:
time: 28.7 us; the launch traced here: 28.6 us
  Pallas kernels  28.6 us (100%)
    pallas_call x1, Pallas kernels, body(): pl.pallas_call(functools.partial(kernel, size_x, size_y), out_shape=(plan...  26.6 us
    pallas_call x1, Pallas kernels, body(): pl.pallas_call(finish, out_shape=jax.ShapeDtypeStruct(field.shape, jnp.fl...  2 us

profile of v2, /device:TPU:121, one launch (start us, length us, event | category | flops | bytes accessed | tf_op | source)
XLA Modules:
  0.0 28.6 jit_solution(17590276282230750549)
XLA Ops:
  0.0 26.6 %multigrid.1 = (f32[48,2,48,128]{3,2,1,0:T(8,128)S(1)}, f32[28,2,32,128]{3,2,1,0:T(8,128)S(1)}, f32[48,48,256]{2,1,0:T(8,128)S(1)}) custom-call(f32[48,48,256]{2,1,0:T(8,128)} %field.1, f32[48,48,256]{2,1,0:T(8,128)} %stdev.1, f32[4,256,256]{2,1,0:T(8,128)} %mixing.1, f32[4,256]{1,0:T(4,128)} %gen_weight.1), custom_call_target="tpu_custom_call" | custom-call | flops 1398276096 | bytes 8388608 | tf_op jit(solution)/shard_map/multigrid/pallas_call | solution.py:462
  26.6 2.0 %finish.1 = f32[48,48,256]{2,1,0:T(8,128)} custom-call(f32[48,2,48,128]{3,2,1,0:T(8,128)S(1)} %get-tuple-element.8.d0, f32[28,2,32,128]{3,2,1,0:T(8,128)S(1)} %get-tuple-element.9.d1, f32[48,48,256]{2,1,0:T(8,128)S(1)} %get-tuple-element.10.sd), custom_call_target="tpu_custom_call" | custom-call | tf_op jit(solution)/shard_map/finish/pallas_call | solution.py:489

commit v3 on v2

--- a/solution.py
+++ b/solution.py
@@ -229,8 +229,8 @@
         gather_x: (0, 1),
         gather_y: (2, 3),
         gather_corner: (2, 3, 6, 7),
-        gather_0: (0, 1, 4, 5, 6, 7),
-        scatter: (0, 1, 2, 3, 4, 5, 6, 7),
+        gather_0: (4, 5, 6, 7, 0, 1),
+        scatter: (4, 5, 6, 7, 0, 1, 2, 3),
     }
     open_sends, open_receives = [], []
 
@@ -427,20 +427,20 @@
 
 def finish(d0, d1, sd, out, t1, rows, sems):
     copies = []
-    for part in range(6):
-        first = 0 if part == 0 else 4 * part + 4
-        prolong_cols(d1, t1, 4 * part + 8 - first, 24, False, first)
+    for part in range(12):
+        first = 0 if part == 0 else 2 * part + 4
+        prolong_cols(d1, t1, 2 * part + 6 - first, 24, False, first)
 
         def step(j, part=part):
-            m = 4 * part + j
+            m = 2 * part + j
             for half in range(2):
                 lanes = slice(half * LANE, (half + 1) * LANE)
                 even, odd = prolong_rows(t1, m, half, False)
                 rows[2 * m, :, lanes] = (d0[2 * m, half] + even) * sd[2 * m, :, lanes]
                 rows[2 * m + 1, :, lanes] = (d0[2 * m + 1, half] + odd) * sd[2 * m + 1, :, lanes]
 
-        loop(4, step, 2)
-        some = pl.ds(8 * part, 8)
+        loop(2, step, 2)
+        some = pl.ds(4 * part, 4)
         copies.append(pltpu.make_async_copy(rows.at[some], out.at[some], sems.at[part]))
         copies[-1].start()
     for copy in copies:
@@ -491,7 +491,7 @@
             out_shape=jax.ShapeDtypeStruct(field.shape, jnp.float32),
             in_specs=[held] * 3,
             out_specs=pl.BlockSpec(memory_space=pl.ANY),
-            scratch_shapes=[planes(28, 48), vmem(*field.shape), pltpu.SemaphoreType.DMA((6,))],
+            scratch_shapes=[planes(28, 48), vmem(*field.shape), pltpu.SemaphoreType.DMA((12,))],
             compiler_params=pltpu.CompilerParams(vmem_limit_bytes=12 * 2**20),
             name="finish",
         )(*[pltpu.with_memory_space_constraint(a, pltpu.VMEM) for a in parts])

time: 28.7 us -> 28.4 us (0.990)
  Pallas kernels: 28.6 us -> 28.3 us
where the time goes in v3:
time: 28.4 us; the launch traced here: 28.3 us
  Pallas kernels  28.3 us (100%)
    pallas_call x1, Pallas kernels, body(): pl.pallas_call(functools.partial(kernel, size_x, size_y), out_shape=(plan...  26.4 us
    pallas_call x1, Pallas kernels, body(): pl.pallas_call(finish, out_shape=jax.ShapeDtypeStruct(field.shape, jnp.fl...  1.87 us

profile of v3, /device:TPU:121, one launch (start us, length us, event | category | flops | bytes accessed | tf_op | source)
XLA Modules:
  0.0 28.3 jit_solution(4785842954429097315)
XLA Ops:
  0.0 26.4 %multigrid.1 = (f32[48,2,48,128]{3,2,1,0:T(8,128)S(1)}, f32[28,2,32,128]{3,2,1,0:T(8,128)S(1)}, f32[48,48,256]{2,1,0:T(8,128)S(1)}) custom-call(f32[48,48,256]{2,1,0:T(8,128)} %field.1, f32[48,48,256]{2,1,0:T(8,128)} %stdev.1, f32[4,256,256]{2,1,0:T(8,128)} %mixing.1, f32[4,256]{1,0:T(4,128)} %gen_weight.1), custom_call_target="tpu_custom_call" | custom-call | flops 1398276096 | bytes 8388608 | tf_op jit(solution)/shard_map/multigrid/pallas_call | solution.py:462
  26.4 1.9 %finish.1 = f32[48,48,256]{2,1,0:T(8,128)} custom-call(f32[48,2,48,128]{3,2,1,0:T(8,128)S(1)} %get-tuple-element.8.d0, f32[28,2,32,128]{3,2,1,0:T(8,128)S(1)} %get-tuple-element.9.d1, f32[48,48,256]{2,1,0:T(8,128)S(1)} %get-tuple-element.10.sd), custom_call_target="tpu_custom_call" | custom-call | tf_op jit(solution)/shard_map/finish/pallas_call | solution.py:489
